TPU v7x, 32 devices: a whole 2x2x4 slice. The times are simulated.
32 devices in a mesh: amp: 8 (over z, x), int: 4 (over y, core).
Axes of the slice: x: 2, y: 2, z: 4, core: 2. Of those that a mesh axis runs over, the one named last changes fastest.
Arguments:
- t2_stored: float32 [1024, 4096], P('amp', 'int'), may hold values from -6 to 6
- integrals: float32 [4096, 4096], P('amp', 'int'), may hold values from -0.09375 to 0.09375
- driver: float32 [1024, 4096], P('amp', 'int'), may hold values from -6 to 6
- eps_occ: float32 [120], replicated, may hold values from -2 to -0.3
- eps_vir: float32 [600], replicated, may hold values from 0.1 to 3
- blk_len: int32 [32], replicated, may hold values from 32 to 128, as said below
- t2_order: int32 [32], replicated, may hold values from 0 to 31, as said below
- int_order: int32 [32], replicated, may hold values from 0 to 31, as said below
Outputs:
- update: float32 [1024, 4096], P('amp', 'int')
Inputs may be any that keep to these rules, and one draw needn't show every extreme that they name: `blk_len`: live slots of a block come first; some block is full and some has 32 live slots. `int_order`: a permutation of the blocks; the integrals' row blocks on one amp index are int_order's blocks of that index. `t2_order`: a permutation of the blocks; the stored column blocks on each int index hold exactly one of the blocks that int_order places on each amp index.
All inputs are finite; a program needn't handle non-finite values.
Results may differ from a plain program's by a relative error of at most 0.00005.
Values sent between devices are 32-bit elements; how exact they have to be, the bound alone decides.
A program may use at most 128 MiB of HBM per device.

v0:
```python
import jax
import jax.numpy as jnp
from jax import lax
from jax.sharding import PartitionSpec as P

NO = 120
NV = 600
TILE = 128


def inverse_of(perm, counter):
    return jnp.sum(jnp.where(perm[None, :] == counter[:, None], counter[None, :], 0), axis=1)


def lookup(table, indices):
    places = jnp.arange(table.shape[0], dtype=jnp.int32)
    return jnp.sum(
        jnp.where(indices[:, None] == places[None, :], table[None, :], jnp.float32(0.0)), axis=1
    )


def on_device(t2_stored, integrals, driver, eps_occ, eps_vir, blk_len, t2_order, int_order):
    row_count = t2_stored.shape[0]
    col_count = integrals.shape[1]
    block_count = blk_len.shape[0]
    owned = integrals.shape[0] // TILE
    per_slice = t2_stored.shape[1] // TILE
    amp_place = lax.axis_index("amp")
    int_place = lax.axis_index("int")
    counter = jnp.arange(block_count, dtype=jnp.int32)
    live_mask = (jnp.arange(TILE, dtype=jnp.int32)[None, :] < blk_len[:, None]).astype(jnp.float32)
    inverse_t2 = inverse_of(t2_order, counter)
    my_blocks = lax.dynamic_slice_in_dim(int_order, amp_place * owned, owned)
    source_block = jnp.take(inverse_t2, my_blocks)
    holder = source_block // per_slice
    all_rows = lax.all_gather(t2_stored, "amp", axis=0, tiled=True)
    here = holder == int_place
    local_pick = jnp.sum(jnp.where(here, source_block % per_slice, 0))
    logical_pick = jnp.sum(jnp.where(here, my_blocks, 0))
    live_row = lax.dynamic_slice_in_dim(live_mask, logical_pick, 1, 0)
    piece = lax.dynamic_slice_in_dim(all_rows, local_pick * TILE, TILE, 1) * live_row
    collected = lax.all_gather(piece, "int", axis=1, tiled=True)
    stacked = collected.reshape(collected.shape[0], owned, TILE)
    amplitudes = jnp.take(stacked, holder, axis=1).reshape(collected.shape[0], owned * TILE)
    summed = lax.psum_scatter(
        jnp.dot(
            amplitudes,
            integrals,
            precision=lax.Precision.HIGHEST,
            preferred_element_type=jnp.float32,
        ),
        "amp",
        scatter_dimension=0,
        tiled=True,
    )
    residual = driver + summed
    row_ids = amp_place * row_count + jnp.arange(row_count, dtype=jnp.int32)
    col_ids = int_place * col_count + jnp.arange(col_count, dtype=jnp.int32)
    occ_first = lookup(eps_occ, row_ids // NO)
    occ_second = lookup(eps_occ, row_ids % NO)
    vir_first = lookup(eps_vir, col_ids % NV)
    vir_second = lookup(eps_vir, (3 * col_ids + col_ids // NV) % NV)
    denominators = (
        vir_first[None, :] + vir_second[None, :] - occ_first[:, None] - occ_second[:, None]
    )
    live_cols = lax.dynamic_slice_in_dim(
        live_mask.reshape(block_count * TILE), int_place * col_count, col_count
    )
    return residual * live_cols[None, :] / denominators


def solution(mesh):
    placed = (P("amp", "int"), P("amp", "int"), P("amp", "int"), P(), P(), P(), P(), P())
    return jax.shard_map(
        on_device, mesh=mesh, in_specs=placed, out_specs=P("amp", "int"), check_vma=False
    )
```

profile of v0, /device:TPU:0, one launch (start us, length us, event | category | flops | bytes accessed | tf_op | source)
XLA Modules:
  0.0 226.4 jit_solution(14133576417330878228)
XLA Ops:
  6.5 2.2 copy.12
  8.7 0.0 all-gather.3.cloned.1.call-update
  8.8 0.0 all-gather.5.cloned.1.call-start
  8.8 0.7 compare_select_fusion.1
  9.6 0.8 select_reduce_fusion.4
  10.3 0.6 gather_fusion
  11.0 0.1 compare_and_fusion
  11.1 0.7 fusion.9
  14.3 0.1 fusion.1
  14.4 72.8 %all-gather.3.cloned.1.call-done = f32[1024,1024]{0,1:T(8,128)} async-done(((f32[128,1024]{0,1:T(8,128)}), f32[1024,1024]{0,1:T(8,128)}) %all-gather.3.cloned.1.call-update) | async-done | bytes 4194320 | tf_op jit(solution)/shard_map/all_gather | solution.py:36
  87.2 1.9 dynamic-slice_multiply_fusion
  89.1 0.0 reduce-scatter.2.cloned.1.call-start
  89.2 0.1 broadcast_bitcast_fusion
  89.3 20.8 %all-gather.5.cloned.1.call-done = f32[1024,512]{0,1:T(8,128)} async-done(((f32[1024,128]{0,1:T(8,128)}), f32[1024,512]{0,1:T(8,128)}) %all-gather.5.cloned.1.call-update) | async-done | bytes 2097168 | tf_op jit(solution)/shard_map/all_gather | solution.py:42
  110.0 2.9 %copy.13 = f32[1024,4,128]{2,0,1:T(8,128)} copy(f32[1024,4,128]{0,2,1:T(8,128)} %bitcast.13) | data formatting | bytes 4194304 | tf_op jit(solution)/shard_map/reshape | solution.py:43
  113.0 3.6 %gather_fusion.1 = f32[4,1024,128]{2,1,0:T(8,128)} fusion(f32[1024,4,128]{2,0,1:T(8,128)} %copy.13, s32[1024]{0:T(1024)S(1)} %pad_clamp_fusion), kind=kCustom, calls=%fused_computation.1 | custom fusion | bytes 4194320 | tf_op jit(solution)/shard_map/jit(_take)/gather | solution.py:44
  116.6 2.9 %copy.14 = f32[1024,4,128]{0,2,1:T(8,128)} copy(f32[1024,4,128]{2,0,1:T(8,128)} %bitcast.12) | data formatting | bytes 4194304 | tf_op jit(solution)/shard_map/jit(_take)/gather | solution.py:44
  119.5 1.8 bitcast_select_fusion
  121.3 8.4 %fusion.12 = f32[1024,1024]{1,0:T(8,128)} fusion(f32[1024,512]{0,1:T(8,128)S(1)} %bitcast_select_fusion, f32[512,1024]{1,0:T(8,128)S(1)} %copy-done), kind=kOutput, calls=%fused_computation.51 | convolution fusion | flops 6442450944 | bytes 8388608 | tf_op jit(solution)/shard_map/dot_general | solution.py:46
  129.8 0.6 copy-done.2
  130.4 0.6 select_reduce_fusion
  131.1 0.1 select_reduce_fusion.3
  131.2 86.6 %reduce-scatter.2.cloned.1.call-done = f32[128,1024]{1,0:T(8,128)} async-done(((f32[1024,1024]{1,0:T(8,128)}), f32[128,1024]{1,0:T(8,128)}) %reduce-scatter.2.cloned.1.call-update) | async-done | bytes 524304 | tf_op jit(solution)/shard_map/reduce_scatter | solution.py:45
  217.8 2.0 subtract_divide_fusion
  (21 shorter events, 0.1 us)
Async XLA Ops:
  6.5 114.8 %copy-start = (f32[512,1024]{1,0:T(8,128)S(1)}, f32[512,1024]{1,0:T(8,128)}, u32[]{:S(2)}) copy-start(f32[512,1024]{1,0:T(8,128)} %param.9) | copy-start | bytes 6291460
  6.5 4.4 %copy-start.3 = (s32[32]{0:T(128)S(1)}, s32[32]{0:T(128)}, u32[]{:S(2)}) copy-start(s32[32]{0:T(128)} %param.15) | copy-start | bytes 388
  6.5 7.7 %copy-start.4 = (s32[32]{0:T(128)S(1)}, s32[32]{0:T(128)}, u32[]{:S(2)}) copy-start(s32[32]{0:T(128)} %param.13) | copy-start | bytes 388
  6.5 80.6 %all-gather.3.cloned.1.call-start = ((), (), s32[]{:S(2)}) async-start(), calls=%async_computation.1 | async-start | bytes 4718592 | tf_op jit(solution)/shard_map/all_gather | solution.py:36
  8.8 101.3 %all-gather.5.cloned.1.call-start = ((), (), s32[]{:S(2)}) async-start(), calls=%async_computation.2 | async-start | bytes 2621440 | tf_op jit(solution)/shard_map/all_gather | solution.py:42
  89.1 128.7 %reduce-scatter.2.cloned.1.call-start = ((), (), s32[]{:S(2)}) async-start(), calls=%async_computation.3 | async-start | bytes 4718592 | tf_op jit(solution)/shard_map/reduce_scatter | solution.py:45
  129.7 0.7 copy-start.2
  129.7 1.4 copy-start.5
  129.7 88.1 %copy-start.1 = (f32[128,1024]{1,0:T(8,128)S(1)}, f32[128,1024]{1,0:T(8,128)}, u32[]{:S(2)}) copy-start(f32[128,1024]{1,0:T(8,128)} %param.10) | copy-start | bytes 1572868
Sparse Core Ops, SparseCore 0:
  9.4 77.7 all-gather.2
  89.2 20.7 all-gather.4
  129.9 87.9 reduce-scatter.1
where the time goes:
time: 227 us; the launch traced here: 226 us
  waiting for transfers between devices  180 us (79%)
  between operations  15.7 us (7%)
  local copies, waits for them, and re-layouts  13 us (6%)
  other arithmetic  8.96 us (4%)
  matrix products  8.4 us (4%)
    reduce_scatter x1, waiting for transfers between devices, on_device(): lax.psum_scatter(jnp.dot(amplitudes, integrals, precision=lax.Precision.H...  86.6 us
    all_gather x1, waiting for transfers between devices, on_device(): all_rows = lax.all_gather(t2_stored, 'amp', axis=0, tiled=True)  72.8 us
    all_gather x1, waiting for transfers between devices, on_device(): collected = lax.all_gather(piece, 'int', axis=1, tiled=True)  20.8 us
    dot_general x1, matrix products, on_device(): jnp.dot(amplitudes, integrals, precision=lax.Precision.HIGHEST, preferred...  8.4 us
    gather x2, local copies, waits for them, and re-layouts, on_device(): jnp.take(stacked, holder, axis=1).reshape(collected.shape[0], owned * TILE)  6.51 us
  transfers between devices with their start and end apart: 3, of which 3 were waited for; matrix products, arithmetic and copies ran while one was open for 2% of the time, Pallas kernels for 0%

commit v1 on v0

--- a/solution.py
+++ b/solution.py
@@ -39,7 +39,9 @@
     logical_pick = jnp.sum(jnp.where(here, my_blocks, 0))
     live_row = lax.dynamic_slice_in_dim(live_mask, logical_pick, 1, 0)
     piece = lax.dynamic_slice_in_dim(all_rows, local_pick * TILE, TILE, 1) * live_row
-    collected = lax.all_gather(piece, "int", axis=1, tiled=True)
+    collected = jnp.concatenate(
+        lax.all_to_all(jnp.stack([piece] * lax.axis_size("int")), "int", 0, 0), axis=1
+    )
     stacked = collected.reshape(collected.shape[0], owned, TILE)
     amplitudes = jnp.take(stacked, holder, axis=1).reshape(collected.shape[0], owned * TILE)
     summed = lax.psum_scatter(

time: 227 us -> 230 us (1.013)
  starting transfers between devices: 0.09 us -> 4.48 us
  local copies, waits for them, and re-layouts: 13 us -> 9.31 us
    all_to_all x0 -> x1, waiting for transfers between devices: none -> 25.6 us  [on_device(): lax.all_to_all(jnp.stack([piece] * lax.axis_size('int')), 'int', 0, 0)]
    all_gather x1 -> x0, waiting for transfers between devices: 20.8 us -> none  [on_device(): collected = lax.all_gather(piece, 'int', axis=1, tiled=True)]
    all_to_all x0 -> x1, starting transfers between devices: none -> 4.44 us  [on_device(): lax.all_to_all(jnp.stack([piece] * lax.axis_size('int')), 'int', 0, 0)]
    reshape x1 -> x0, local copies, waits for them, and re-layouts: 2.94 us -> none  [on_device(): stacked = collected.reshape(collected.shape[0], owned, TILE)]
    reduce_scatter x1, waiting for transfers between devices: 86.6 us -> 84 us  [on_device(): lax.psum_scatter(jnp.dot(amplitudes, integrals, precision=lax.Precision.H...]
  transfers between devices with their start and end apart: 3 -> 3, of which waited for: 3 -> 3; matrix products, arithmetic and copies ran while one was open for 2% -> 3% of each run, Pallas kernels for 0% -> 0%
where the time goes in v1:
time: 230 us; the launch traced here: 229 us
  waiting for transfers between devices  181 us (79%)
  between operations  16.1 us (7%)
  other arithmetic  10 us (4%)
  local copies, waits for them, and re-layouts  9.31 us (4%)
  matrix products  8.4 us (4%)
  starting transfers between devices  4.48 us (2%)
    reduce_scatter x1, waiting for transfers between devices, on_device(): lax.psum_scatter(jnp.dot(amplitudes, integrals, precision=lax.Precision.H...  84 us
    all_gather x1, waiting for transfers between devices, on_device(): all_rows = lax.all_gather(t2_stored, 'amp', axis=0, tiled=True)  70.8 us
    all_to_all x1, waiting for transfers between devices, on_device(): lax.all_to_all(jnp.stack([piece] * lax.axis_size('int')), 'int', 0, 0)  25.6 us
    dot_general x1, matrix products, on_device(): jnp.dot(amplitudes, integrals, precision=lax.Precision.HIGHEST, preferred...  8.4 us
    gather x2, local copies, waits for them, and re-layouts, on_device(): jnp.take(stacked, holder, axis=1).reshape(collected.shape[0], owned * TILE)  6.51 us
  transfers between devices with their start and end apart: 3, of which 3 were waited for; matrix products, arithmetic and copies ran while one was open for 3% of the time, Pallas kernels for 0%

profile of v1, /device:TPU:0, one launch (start us, length us, event | category | flops | bytes accessed | tf_op | source)
XLA Modules:
  0.0 229.4 jit_solution(1337309586038898925)
XLA Ops:
  6.5 0.7 all-gather.2.cloned.1.call-update
  7.3 0.7 compare_select_fusion.1
  8.0 0.8 select_reduce_fusion.4
  8.8 0.6 gather_fusion
  9.4 0.7 compare_and_fusion
  10.2 1.4 fusion.9
  14.1 0.7 fusion.1
  14.8 70.8 %all-gather.2.cloned.1.call-done = f32[1024,1024]{1,0:T(8,128)} async-done(((f32[128,1024]{1,0:T(8,128)}), f32[1024,1024]{1,0:T(8,128)}) %all-gather.2.cloned.1.call-update) | async-done | bytes 4194320 | tf_op jit(solution)/shard_map/all_gather | solution.py:36
  85.6 1.1 dynamic-slice_multiply_fusion
  86.7 1.4 stack.2
  88.1 4.4 %all-to-all-start = ((f32[4,1024,128]{2,1,0:T(8,128)}), f32[4,1024,128]{2,1,0:T(8,128)}, u32[]{:S(2)}, u32[]{:S(2)}) async-start(f32[4,1024,128]{2,1,0:T(8,128)} %stack.2), calls=%async_computation | async-start | bytes 4194304 | tf_op jit(solution)/shard_map/all_to_all | solution.py:43
  92.6 0.0 reduce-scatter.2.cloned.1.call-start
  92.6 0.1 broadcast_bitcast_fusion
  92.7 25.6 %all-to-all-done = f32[4,1024,128]{2,1,0:T(8,128)} async-done(((f32[4,1024,128]{2,1,0:T(8,128)}), f32[4,1024,128]{2,1,0:T(8,128)}, u32[]{:S(2)}, u32[]{:S(2)}) %all-to-all-start) | async-done | bytes 2097184 | tf_op jit(solution)/shard_map/all_to_all | solution.py:43
  118.3 3.6 %gather_fusion.1 = f32[4,1024,128]{2,1,0:T(8,128)} fusion(f32[1024,4,128]{2,0,1:T(8,128)} %bitcast.2, s32[1024]{0:T(1024)S(1)} %pad_clamp_fusion), kind=kCustom, calls=%fused_computation.1 | custom fusion | bytes 4194320 | tf_op jit(solution)/shard_map/jit(_take)/gather | solution.py:46
  121.9 2.9 %copy.10 = f32[1024,4,128]{0,2,1:T(8,128)} copy(f32[1024,4,128]{2,0,1:T(8,128)} %bitcast.12) | data formatting | bytes 4194304 | tf_op jit(solution)/shard_map/jit(_take)/gather | solution.py:46
  124.8 1.8 bitcast_select_fusion
  126.7 8.4 %fusion.12 = f32[1024,1024]{1,0:T(8,128)} fusion(f32[1024,512]{0,1:T(8,128)S(1)} %bitcast_select_fusion, f32[512,1024]{1,0:T(8,128)S(1)} %copy-done), kind=kOutput, calls=%fused_computation.51 | convolution fusion | flops 6442450944 | bytes 8388608 | tf_op jit(solution)/shard_map/dot_general | solution.py:48
  135.1 0.0 reduce-scatter.2.cloned.1.call-update
  135.1 0.6 copy-done.2
  135.7 0.6 select_reduce_fusion
  136.5 0.1 select_reduce_fusion.3
  136.6 84.0 %reduce-scatter.2.cloned.1.call-done = f32[128,1024]{1,0:T(8,128)} async-done(((f32[1024,1024]{1,0:T(8,128)}), f32[128,1024]{1,0:T(8,128)}) %reduce-scatter.2.cloned.1.call-update) | async-done | bytes 524304 | tf_op jit(solution)/shard_map/reduce_scatter | solution.py:47
  220.5 2.0 subtract_divide_fusion
  (15 shorter events, 0.1 us)
Async XLA Ops:
  6.5 120.1 %copy-start = (f32[512,1024]{1,0:T(8,128)S(1)}, f32[512,1024]{1,0:T(8,128)}, u32[]{:S(2)}) copy-start(f32[512,1024]{1,0:T(8,128)} %param.9) | copy-start | bytes 6291460
  6.5 79.1 %all-gather.2.cloned.1.call-start = ((), (), s32[]{:S(2)}) async-start(), calls=%async_computation.2 | async-start | bytes 4718592 | tf_op jit(solution)/shard_map/all_gather | solution.py:36
  88.1 30.2 %all-to-all-start = ((f32[4,1024,128]{2,1,0:T(8,128)}), f32[4,1024,128]{2,1,0:T(8,128)}, u32[]{:S(2)}, u32[]{:S(2)}) async-start(f32[4,1024,128]{2,1,0:T(8,128)} %stack.2), calls=%async_computation | async-start | bytes 4194304 | tf_op jit(solution)/shard_map/all_to_all | solution.py:43
  92.6 127.9 %reduce-scatter.2.cloned.1.call-start = ((), (), s32[]{:S(2)}) async-start(), calls=%async_computation.3 | async-start | bytes 4718592 | tf_op jit(solution)/shard_map/reduce_scatter | solution.py:47
  135.1 0.7 copy-start.2
  135.1 1.4 copy-start.3
  135.1 85.4 %copy-start.1 = (f32[128,1024]{1,0:T(8,128)S(1)}, f32[128,1024]{1,0:T(8,128)}, u32[]{:S(2)}) copy-start(f32[128,1024]{1,0:T(8,128)} %param.10) | copy-start | bytes 1572868
Sparse Core Ops, SparseCore 0:
  9.5 76.0 all-gather.1
  135.2 85.2 reduce-scatter.1
